TPU v7x, 32 devices: a whole 2x2x4 slice. The times are simulated.
32 devices in a mesh: dom: 8 (over z, y), brick: 4 (over x, core).
Axes of the slice: x: 2, y: 2, z: 4, core: 2. Of those that a mesh axis runs over, the one named last changes fastest.
Arguments:
- features: bfloat16 [65536, 256], P(('dom', 'brick')), may hold values from -6 to 6
- elem_owner: int32 [65536, 1], P(('dom', 'brick')), may hold values from 0 to 31; in each aligned block of 2048 rows (0 to 2047, 2048 to 4095, ...) at most 128 rows name the same one
- elem_voxel: int32 [65536], P(('dom', 'brick')), may hold values from 0 to 16383
- w_first: bfloat16 [256, 256], replicated, may hold values from -0.375 to 0.375
- b_first: float32 [256], replicated, may hold values from -3 to 3
- w_conv: bfloat16 [3, 3, 3, 256, 128], replicated, may hold values from -0.078125 to 0.078125
- cotangent: bfloat16 [8, 16, 16, 32, 128], P('dom', None, None, 'brick'), may hold values from -6 to 6
Outputs:
- volume_out: bfloat16 [8, 16, 16, 32, 128], P('dom', None, None, 'brick')
- conv_grad: float32 [3, 3, 3, 256, 128], replicated
- w_first_grad: float32 [256, 256], replicated
- b_first_grad: float32 [256], replicated
Inputs may be any that keep to these rules, and one draw needn't show every extreme that they name: `elem_owner`: within the rows of one device, at most 128 rows name the same owner.
All inputs are finite; a program needn't handle non-finite values.
Results may differ from a plain program's by a relative error of at most 0.0065.
Values may be sent and summed in bfloat16 or wider, within the bound.
No kernel may reach another device: no remote copies, remote signals or barrier semaphores. Data moves between devices by JAX's collectives and lax.ppermute only.
A program may use at most 128 MiB of HBM per device.

v0:
```python
import functools
import math

import jax
import jax.numpy as jnp
from jax import lax
from jax.experimental import pallas as pl
from jax.experimental.pallas import tpu as pltpu
from jax.sharding import PartitionSpec as P

BF16 = jnp.bfloat16
F32 = jnp.float32
LANES = 128
PAD = 16
VMEM = pl.BlockSpec(memory_space=pltpu.VMEM)
BIG = 56 * 2**20
SMALL = 24 * 2**20
ANY = pl.BlockSpec(memory_space=pl.ANY)


def lasting(microseconds):
    return pl.CostEstimate(
        flops=int(microseconds * 1.1e9), bytes_accessed=int(microseconds * 3.5e6), transcendentals=0
    )


def dot(a, b):
    return jnp.dot(a, b, preferred_element_type=F32)


def dot_nt(a, b):
    return lax.dot_general(a, b, (((1,), (1,)), ((), ())), preferred_element_type=F32)


def dot_tn(a, b):
    return lax.dot_general(a, b, (((0,), (0,)), ((), ())), preferred_element_type=F32)


def shifts_of(parity):
    return [s for s in range(8) if s & ~parity == 0]


def offset_of(parity, shift):
    index = 0
    for bit in (4, 2, 1):
        index = 3 * index + (1 if not parity & bit else 0 if shift & bit else 2)
    return index


def pack_kernel(group, cap, dims, half_ref, owner_ref, voxel_ref, feat_ref, out_ref, slot_ref, table_ref):
    rows = feat_ref.shape[0]
    devices = table_ref.shape[0] // 2
    half_x, half_y, half_z = dims
    cells = half_x * half_y * half_z
    first_device = half_ref[0] * devices
    step = 2 * LANES

    @pl.when(pl.program_id(0) == 0)
    def _():
        before = lax.broadcasted_iota(jnp.int32, (step, step), 0) < lax.broadcasted_iota(
            jnp.int32, (step, step), 1
        )
        before = before.astype(F32).astype(BF16)
        device = lax.broadcasted_iota(jnp.int32, (devices, step), 0)
        place = lax.broadcasted_iota(jnp.int32, (LANES, step), 0).astype(F32)
        seen = jnp.zeros((devices, 1), F32)
        table = jnp.zeros((2 * devices, LANES), F32)
        for start in range(0, rows, step):
            here = (device == owner_ref[:, start : start + step] - first_device).astype(F32)
            rank = here * (dot(here.astype(BF16), before) + seen + 1.0)
            slot = jnp.sum(rank + here * (device * cap).astype(F32), axis=0, keepdims=True) - 1.0
            slot_ref[:, start : start + step] = slot.astype(jnp.int32)
            seen = seen + jnp.sum(here, axis=1, keepdims=True)
            voxel = voxel_ref[:, start : start + step]
            z, line = voxel % (2 * half_z), voxel // (2 * half_z)
            y, x = line % (2 * half_y), line // (2 * half_y)
            parity = (x % 2) * 4 + (y % 2) * 2 + z % 2
            code = parity * cells + ((x // 2) * half_y + y // 2) * half_z + z // 2
            high, low = (code >> 7) + 1, code & 127
            values = jnp.concatenate([here * high.astype(F32), here * low.astype(F32)], axis=0)
            ranked = jnp.where(place == jnp.sum(rank, axis=0, keepdims=True) - 1.0, 1.0, 0.0)
            table = table + dot_nt(values.astype(BF16), ranked.astype(BF16))
        table_ref[...] = table

    first = pl.program_id(0) * group
    place = lax.broadcasted_iota(jnp.int32, (group * cap, rows), 0) + first * cap
    chosen = jnp.where(place == slot_ref[...], 1.0, 0.0).astype(BF16)
    packed = dot(chosen, feat_ref[...]).astype(BF16)
    for g in range(group):
        out_ref[g, :cap, :] = packed[g * cap : (g + 1) * cap]
        high = table_ref[pl.ds(first + g, 1), :]
        low = table_ref[pl.ds(devices + first + g, 1), :]
        both = jnp.concatenate([high, low], axis=1)
        out_ref[g, cap:, :] = jnp.broadcast_to(both, (PAD, 2 * LANES)).astype(BF16)


def pack(half, owner, voxel, features, cap, devices, dims):
    rows, width = features.shape
    group = max(1, 512 // cap)
    return pl.pallas_call(
        functools.partial(pack_kernel, group, cap, dims),
        out_shape=jax.ShapeDtypeStruct((devices, cap + PAD, width), BF16),
        grid_spec=pltpu.PrefetchScalarGridSpec(
            num_scalar_prefetch=1,
            grid=(devices // group,),
            in_specs=[VMEM] * 3,
            out_specs=pl.BlockSpec((group, cap + PAD, width), lambda i, half: (i, 0, 0)),
            scratch_shapes=[pltpu.VMEM((1, rows), jnp.int32), pltpu.VMEM((2 * devices, LANES), F32)],
        ),
        compiler_params=pltpu.CompilerParams(vmem_limit_bytes=BIG),
        cost_estimate=lasting(4),
        name="pack",
    )(half, owner, voxel, features)


def lay_out(cot_ref, dims, wide, tall):
    half_x, half_y, half_z = dims
    cells = half_x * half_y * half_z
    width = cot_ref.shape[1]
    same = cot_ref[:cells, :].astype(F32)
    above = jnp.broadcast_to(cot_ref[cells:, :].astype(F32)[:, None, :], (cells // half_z, half_z, width))
    highest = lax.broadcasted_iota(jnp.int32, (cells, width), 0) % half_z == half_z - 1
    ahead = jnp.where(highest, above.reshape(cells, width), pltpu.roll(same, cells - 1, 0))
    for shift in range(8):
        values = ahead if shift & 1 else same
        if shift & 4:
            gap = half_y * half_z
            values = jnp.concatenate([values[gap:], jnp.zeros((gap, width), F32)], axis=0)
        if shift & 2:
            values = values.reshape(half_x, half_y * half_z, width)
            gone = jnp.zeros((half_x, half_z, width), F32)
            values = jnp.concatenate([values[:, half_z:], gone], axis=1).reshape(cells, width)
        if wide is not None:
            wide[:, shift * width : (shift + 1) * width] = values.astype(BF16)
        if tall is not None:
            tall[shift * width : (shift + 1) * width, :] = values.T.astype(BF16)


def codes_of(recv, cap, vox_count):
    parts = recv[:, cap, :].astype(jnp.int32)
    high, low = parts[:, :cap], parts[:, LANES : LANES + cap]
    return jnp.where(high > 0, (high - 1) * 128 + low, vox_count).reshape(-1)


def put_rows(ref, start, values):
    count = values.shape[0]
    ref[pl.ds(2 * start, count, stride=2), :] = values[:, :LANES]
    ref[pl.ds(2 * start + 1, count, stride=2), :] = values[:, LANES:]


def get_rows(ref, start, count):
    low = ref[pl.ds(2 * start, count, stride=2), :]
    high = ref[pl.ds(2 * start + 1, count, stride=2), :]
    return low, high


UNROLL = 16
CHUNK = 512


def pairs_of(ref):
    return ref.reshape(ref.shape[0] // 2, 2, LANES)


def add_products(block, conv_ref, parity, dims, same, next_):
    half_x, half_y, half_z = dims
    plane = half_y * half_z
    width = conv_ref.shape[2]
    shifts = shifts_of(parity)
    right = jnp.concatenate([conv_ref[offset_of(parity, s)] for s in shifts], axis=1)
    product = dot(block, right)
    for at, s in enumerate(shifts):
        part = product[:, at * width : (at + 1) * width].reshape(half_x, plane, width)
        dx = 1 if s & 4 else 0
        dy = half_z if s & 2 else 0
        total = next_ if s & 1 else same
        total[dx:, dy:, :] += part[: half_x - dx, : plane - dy, :]


def shifted_along_z(same, next_, dims):
    half_x, half_y, half_z = dims
    cells = half_x * half_y * half_z
    width = same.shape[2]
    after = next_[...].reshape(cells, width)
    lowest = lax.broadcasted_iota(jnp.int32, (cells, width), 0) % half_z == 0
    total = same[...].reshape(cells, width) + jnp.where(lowest, 0.0, pltpu.roll(after, 1, 0))
    return total, after.reshape(cells // half_z, half_z, width)[:, half_z - 1, :]


def slab_kernel(cap, scale, dims, kind, *refs):
    ahead, back, far = kind != "far_back", kind != "far_ahead", kind != "near"
    bit, codes, recv_ref, w_ref, b_ref, cot_ref, conv_hbm = refs[:7]
    wide = tall = slopes = None
    if kind == "near":
        out_ref, edge_ref, terms_hbm, wgrad, bgrad, sums, rows, conv, sems, slopes, wide, tall, terms, same, next_ = refs[7:]
    elif kind == "far_ahead":
        terms_hbm, lent_ref, rest_ref, keep_hbm, send_hbm, sums, rows, conv, sems, tall, terms, flat, same, next_ = refs[7:]
    else:
        wterm_ref, bterm_ref, first_ref, sums, rows, conv, sems, slopes, wide, wgrad, bgrad = refs[7:]
    sources, _, width = recv_ref.shape
    half_x, half_y, half_z = dims
    cells = half_x * half_y * half_z
    vox_count = 8 * cells
    out_width = conv.shape[2]
    count = sources * cap
    loads = [pltpu.make_async_copy(conv_hbm, conv, sems.at[0])]
    if kind == "far_ahead":
        loads.append(pltpu.make_async_copy(terms_hbm, terms, sems.at[1]))
    for load in loads:
        load.start()
    lay_out(cot_ref, dims, wide, tall)
    step = CHUNK // cap
    sum_rows, new_rows = pairs_of(sums), pairs_of(rows)

    def layer(i, _):
        feats = recv_ref[pl.ds(i * step, step), :cap, :].reshape(CHUNK, width)
        pre = dot(feats, w_ref[...]) + b_ref[...]
        sig = jax.nn.sigmoid(pre)
        if ahead:
            put_rows(rows, i * CHUNK, (pre * sig).astype(BF16).astype(F32))
        if back:
            slopes[pl.ds(i * CHUNK, CHUNK), :] = sig * (1.0 + pre * (1.0 - sig))
        return 0

    lax.fori_loop(0, count // CHUNK, layer, 0)
    if ahead:

        def clear(i, _):
            sums[pl.ds(pl.multiple_of(i * 1024, 1024), 1024), :] = jnp.zeros((1024, LANES), F32)
            return 0

        lax.fori_loop(0, vox_count // 512, clear, 0)

        def add(i, _):
            for u in range(0, UNROLL, 2):
                at = i * UNROLL + u
                a, b = codes[at], codes[at + 1]
                old_a, old_b = sum_rows[a], sum_rows[b]
                new_a = old_a + new_rows[at]
                new_b = jnp.where(a == b, new_a, old_b) + new_rows[at + 1]
                sum_rows[a] = new_a
                sum_rows[b] = new_b
            return 0

        lax.fori_loop(0, count // UNROLL, add, 0)
    for load in loads:
        load.wait()
    if ahead:
        same[...] = jnp.zeros_like(same)
        next_[...] = jnp.zeros_like(next_)
    stores = []
    for parity in range(8):
        shifts = shifts_of(parity)
        if ahead:
            low, high = get_rows(sums, parity * cells, cells)
            block = jnp.concatenate([low.astype(BF16), high.astype(BF16)], axis=1)
            left = jnp.concatenate([tall[s * out_width : (s + 1) * out_width, :] for s in shifts], axis=0)
            grads = dot(left, block)
            for at, s in enumerate(shifts):
                first = offset_of(parity, s) * width
                grad = grads[at * out_width : (at + 1) * out_width].T
                if far:
                    flat[first : first + width, :] = (grad + terms[first : first + width, :]).astype(BF16)
                else:
                    terms[first : first + width, :] = grad
            add_products(block, conv, parity, dims, same, next_)
        if back:
            left = jnp.concatenate([wide[:, s * out_width : (s + 1) * out_width] for s in shifts], axis=1)
            right = jnp.concatenate([conv[offset_of(parity, s)] for s in shifts], axis=1)
            put_rows(sums, parity * cells, (dot_nt(left, right) * scale).astype(BF16).astype(F32))
    if kind == "near":
        out_ref[...], edge_ref[...] = shifted_along_z(same, next_, dims)
        stores.append(pltpu.make_async_copy(terms, terms_hbm, sems.at[1]))
        stores[-1].start()
    if kind == "far_ahead":
        size = flat.shape[0] // 2
        mine = pl.multiple_of(bit[0] * size, 16)
        other = pl.multiple_of((1 - bit[0]) * size, 16)
        stores = [
            pltpu.make_async_copy(flat.at[pl.ds(mine, size)], keep_hbm, sems.at[2]),
            pltpu.make_async_copy(flat.at[pl.ds(other, size)], send_hbm, sems.at[3]),
        ]
        for store in stores:
            store.start()
        total, edge = shifted_along_z(same, next_, dims)
        cut = lent_ref.shape[0]
        lent_ref[...] = total[:cut].astype(BF16)
        rest_ref[: cells - cut, :] = total[cut:].astype(BF16)
        rest_ref[cells - cut :, :] = edge.astype(BF16)
    if back:
        sums[2 * vox_count :, :] = jnp.zeros((16, LANES), F32)

        def take(i, _):
            for u in range(UNROLL):
                at = i * UNROLL + u
                new_rows[at] = sum_rows[codes[at]]
            return 0

        lax.fori_loop(0, count // UNROLL, take, 0)
        wgrad[...] = wterm_ref[...] if far else jnp.zeros_like(wgrad)
        bgrad[...] = bterm_ref[...] if far else jnp.zeros_like(bgrad)

        def layer_back(i, _):
            feats = recv_ref[pl.ds(i * step, step), :cap, :].reshape(CHUNK, width)
            low, high = get_rows(rows, i * CHUNK, CHUNK)
            pre_grad = (jnp.concatenate([low, high], axis=1) * slopes[pl.ds(i * CHUNK, CHUNK), :]).astype(BF16)
            wgrad[...] += dot_tn(feats, pre_grad)
            bgrad[...] += jnp.sum(pre_grad.astype(F32), axis=0, keepdims=True)
            return 0

        lax.fori_loop(0, count // CHUNK, layer_back, 0)
    if kind == "far_back":
        first_ref[:width, :] = wgrad[:, :LANES].astype(BF16)
        first_ref[width : 2 * width, :] = wgrad[:, LANES:].astype(BF16)
        bias = bgrad[...]
        row = lax.broadcasted_iota(jnp.int32, (PAD, LANES), 0)
        bias = jnp.where(row == 0, bias[:, :LANES], jnp.where(row == 1, bias[:, LANES:], 0.0))
        first_ref[2 * width : 2 * width + PAD, :] = bias.astype(BF16)
        rest = first_ref.shape[0] - 2 * width - PAD
        first_ref[2 * width + PAD :, :] = jnp.zeros((rest, LANES), BF16)
    for store in stores:
        store.wait()


def slab(kind, bit, codes, recv, w_first, b_first, cot, w_conv, cap, scale, dims, earlier=(), length=None):
    sources, _, width = recv.shape
    half_x, half_y, half_z = dims
    cells = half_x * half_y * half_z
    out_width = w_conv.shape[2]
    n_conv = 27 * width
    count = sources * cap
    operands = (recv, w_first, b_first, cot, w_conv) + tuple(earlier)
    in_specs = [VMEM] * 4 + [ANY]
    scratch = [
        pltpu.VMEM((2 * 8 * cells + 16, LANES), F32),
        pltpu.VMEM((2 * count, LANES), F32),
        pltpu.VMEM(w_conv.shape, BF16),
        pltpu.SemaphoreType.DMA((4,)),
    ]
    slopes = pltpu.VMEM((count, width), F32)
    wide = pltpu.VMEM((cells, 8 * out_width), BF16)
    tall = pltpu.VMEM((8 * out_width, cells), BF16)
    terms = pltpu.VMEM((n_conv, LANES), F32)
    outputs = [pltpu.VMEM((half_x, half_y * half_z, out_width), F32)] * 2
    first_layer = (jax.ShapeDtypeStruct((width, width), F32), jax.ShapeDtypeStruct((1, width), F32))
    if kind == "near":
        out_shape = (
            jax.ShapeDtypeStruct((cells, out_width), F32),
            jax.ShapeDtypeStruct((cells // half_z, out_width), F32),
            jax.ShapeDtypeStruct((n_conv, LANES), F32),
        ) + first_layer
        out_specs = (VMEM, VMEM, ANY, VMEM, VMEM)
        scratch += [slopes, wide, tall, terms] + outputs
    elif kind == "far_ahead":
        in_specs += [ANY]
        lent = (cells + cells // half_z) * 3 // 4
        out_shape = (
            jax.ShapeDtypeStruct((lent, out_width), BF16),
            jax.ShapeDtypeStruct((cells + cells // half_z - lent, out_width), BF16),
            jax.ShapeDtypeStruct((n_conv // 2, LANES), BF16),
            jax.ShapeDtypeStruct((n_conv // 2, LANES), BF16),
        )
        out_specs = (VMEM, VMEM, ANY, ANY)
        scratch += [tall, terms, pltpu.VMEM((n_conv, LANES), BF16)]
        scratch += outputs
    else:
        in_specs += [VMEM, VMEM]
        out_shape = jax.ShapeDtypeStruct((length, LANES), BF16)
        out_specs = VMEM
        scratch += [slopes, wide, pltpu.VMEM((width, width), F32), pltpu.VMEM((1, width), F32)]
    return pl.pallas_call(
        functools.partial(slab_kernel, cap, scale, dims, kind),
        out_shape=out_shape,
        grid_spec=pltpu.PrefetchScalarGridSpec(
            num_scalar_prefetch=2, grid=(1,), in_specs=in_specs, out_specs=out_specs, scratch_shapes=scratch
        ),
        compiler_params=pltpu.CompilerParams(vmem_limit_bytes=BIG),
        cost_estimate=lasting({"near": 26, "far_ahead": 20, "far_back": 11}[kind]),
        name="slab_" + kind,
    )(bit, codes, *operands)


def finish_kernel(scale, n_block, bit_ref, mine_ref, theirs_ref, conv_ref, w_ref, b_ref, first):
    width = w_ref.shape[0]
    n_conv = conv_ref.shape[0] // 8
    n_first = n_block - n_conv

    def write(refs):
        for k in range(8):
            source, at = refs[k // 4], k % 4 * n_block
            conv_ref[k * n_conv : (k + 1) * n_conv, :] = source[at : at + n_conv, :].astype(F32) * scale
            first[k * n_first : (k + 1) * n_first, :] = source[at + n_conv : at + n_block, :].astype(F32)
        w_ref[:, :LANES] = first[:width, :]
        w_ref[:, LANES:] = first[width : 2 * width, :]
        bias = first[2 * width : 2 * width + 8, :]
        b_ref[...] = jnp.concatenate([bias[0:1], bias[1:2]], axis=1)

    @pl.when(bit_ref[0] == 0)
    def _():
        write((mine_ref, theirs_ref))

    @pl.when(bit_ref[0] == 1)
    def _():
        write((theirs_ref, mine_ref))


def finish(bit, mine, theirs, n_conv, width, scale):
    n_block = mine.shape[0] // 4
    return pl.pallas_call(
        functools.partial(finish_kernel, scale, n_block),
        out_shape=(
            jax.ShapeDtypeStruct((n_conv, LANES), F32),
            jax.ShapeDtypeStruct((width, width), F32),
            jax.ShapeDtypeStruct((1, width), F32),
        ),
        grid_spec=pltpu.PrefetchScalarGridSpec(
            num_scalar_prefetch=1,
            grid=(1,),
            in_specs=[VMEM] * 2,
            out_specs=(VMEM,) * 3,
            scratch_shapes=[pltpu.VMEM((8 * n_block - n_conv, LANES), F32)],
        ),
        compiler_params=pltpu.CompilerParams(vmem_limit_bytes=SMALL),
        cost_estimate=lasting(3),
        name="finish",
    )(bit, mine, theirs)


AXES = ("half", "dom", "brick")


def passed_along(array, axis, by):
    size = lax.axis_size(axis)
    pairs = [(i, i + by) for i in range(size) if 0 <= i + by < size]
    return lax.ppermute(array, axis, pairs)


def crossed(array):
    return lax.ppermute(array, "half", [(0, 1), (1, 0)])


def exchange(array, mask):
    return lax.ppermute(array, AXES, [(i, i ^ mask) for i in range(lax.axis_size(AXES))])


def bit_groups():
    bits = lax.axis_size(AXES).bit_length() - 1
    return [(0, 1)] + [(at, min(2, bits - at)) for at in range(1, bits, 2)]


def sent_blocks(part, me, first, count):
    blocks = part.reshape(1 << count, -1, LANES)
    mine = (me >> first) & ((1 << count) - 1)
    arrived = [
        exchange(lax.dynamic_index_in_dim(blocks, mine ^ m, 0, keepdims=False), m << first)
        for m in range(1, 1 << count)
    ]
    return [lax.dynamic_index_in_dim(blocks, mine, 0, keepdims=False)] + arrived


def added(blocks):
    total = blocks[0].astype(F32)
    for block in blocks[1:]:
        total = total + block.astype(F32)
    return total.astype(BF16)


def reduced(part, me, first, count):
    return added(sent_blocks(part, me, first, count))


def gathered(part, me, first, count):
    blocks = [part] + [exchange(part, m << first) for m in range(1, 1 << count)]
    for bit in range(count):
        swap = (me >> (first + bit)) & 1 == 1
        blocks = [jnp.where(swap, blocks[i ^ (1 << bit)], blocks[i]) for i in range(1 << count)]
    return jnp.concatenate(blocks, axis=0)


def shards(features, elem_owner, elem_voxel, w_first, b_first, w_conv, cotangent):
    n_brick = lax.axis_size("brick")
    devices = lax.axis_size(AXES)
    near = devices // 2
    me = lax.axis_index(AXES)
    rows, width = features.shape
    cap = 2 * rows // devices
    dims = cotangent.shape[1:4]
    half_x, half_y, half_z = dims
    cells = half_x * half_y * half_z
    vox_count = 8 * cells
    out_width = cotangent.shape[4]
    scale = 1.0 / math.sqrt(devices * cells)
    bias = b_first.reshape(1, width)
    offsets = w_conv.reshape(27, width, out_width)

    cot = cotangent.reshape(cells, out_width)
    plane = cotangent[0, :, :, 0, :].reshape(-1, out_width)
    above = passed_along(plane, "brick", -1)

    half = lax.axis_index("half").reshape(1)
    owner, voxel = elem_owner.reshape(1, rows), elem_voxel.reshape(1, rows)

    def swapped(packed):
        return lax.all_to_all(packed, ("dom", "brick"), split_axis=0, concat_axis=0, tiled=True)

    near_recv = swapped(pack(half, owner, voxel, features, cap, near, dims))
    far_packed = pack(1 - half, owner, voxel, features, cap, near, dims)
    far_recv = swapped(far_packed)

    n_conv = 27 * width
    unit = 2 * devices
    n_block = -(-(n_conv // 8 + (2 * width + PAD) // 8) // unit) * unit
    n_first = 8 * n_block - n_conv
    bit = (me & 1).reshape(1)
    near_codes = codes_of(near_recv, cap, vox_count)
    cots, near_codes = lax.optimization_barrier((jnp.concatenate([cot, above], axis=0), near_codes))
    far_cots = crossed(cots)
    near_out, near_edge, conv_term, *first_terms = slab(
        "near", bit, near_codes, near_recv, w_first, bias, cots, offsets, cap, scale, dims
    )
    far_codes = codes_of(far_recv, cap, vox_count)
    lent, rest, keep, send = slab(
        "far_ahead", bit, far_codes, far_recv, w_first, bias, far_cots, offsets, cap, scale, dims, (conv_term,)
    )
    lent, rest = crossed(lent), crossed(rest)
    part = added([keep, exchange(send, 1)])
    part, far_codes = lax.optimization_barrier((part, far_codes))
    groups = bit_groups()
    blocks = sent_blocks(part, me, *groups[1])
    first_part = slab(
        "far_back", bit, far_codes, far_recv, w_first, bias, far_cots, offsets, cap, scale, dims, first_terms, n_first
    )
    first_part, lent, blocks = lax.optimization_barrier((first_part, lent, blocks))
    for first, count in groups[:2]:
        first_part = reduced(first_part, me, first, count)
    part, first_part, rest = lax.optimization_barrier((added(blocks), first_part, rest))
    part = jnp.concatenate([part, first_part], axis=0)
    for first, count in groups[2:]:
        part = reduced(part, me, first, count)
    for first, count in reversed(groups[2:]):
        part = gathered(part, me, first, count)
    lent = jnp.concatenate([lent, rest], axis=0).astype(F32)
    part, edge = lax.optimization_barrier((part, near_edge + lent[cells:]))
    below = passed_along(edge, "brick", 1)
    part, below = lax.optimization_barrier((gathered(part, me, *groups[1]), below))
    conv_grad, w_first_grad, b_first_grad = finish(bit, part, exchange(part, 1), n_conv, width, scale)

    below = below.reshape(half_x, half_y, 1, out_width)
    whole = (near_out + lent[:cells]).reshape(half_x, half_y, half_z, out_width)
    volume_out = jnp.concatenate([whole[:, :, :1] + below, whole[:, :, 1:]], axis=2).astype(BF16)
    return (
        volume_out[None],
        conv_grad.reshape(w_conv.shape),
        w_first_grad,
        b_first_grad.reshape(width),
    )


def solution(mesh):
    n_dom, n_brick = mesh.devices.shape
    halves = jax.sharding.Mesh(mesh.devices.reshape(2, n_dom // 2, n_brick), AXES)
    bricks = P(("half", "dom"), None, None, "brick", None)
    return jax.shard_map(
        shards,
        mesh=halves,
        in_specs=(P(AXES, None), P(AXES, None), P(AXES), P(), P(), P(), bricks),
        out_specs=(bricks, P(), P(), P()),
        check_vma=False,
    )
```

profile of v0, /device:TPU:0, one launch (start us, length us, event | category | flops | bytes accessed | tf_op | source)
XLA Modules:
  0.0 160.2 jit_solution(5780926949457490469)
XLA Ops:
  0.6 5.5 %pack.2 = bf16[16,144,256]{2,1,0:T(8,128)(2,1)} custom-call(s32[1]{0:T(128)} %bitcast.3.half_ref, s32[1,2048]{1,0:T(1,128)} %bitcast.81, s32[1,2048]{1,0:T(1,128)} %bitcast.83, bf16[2048,256]{1,0:T(8,128)(2,1)} %feat_ref.3), custom_call_target="tpu_custom_call" | custom-call | flops 4400000000 | bytes 14000000 | tf_op jit(solution)/shard_map/pack/pallas_call | solution.py:100
  6.1 6.4 %all-to-all-start = ((bf16[16,144,256]{2,1,0:T(8,128)(2,1)}), bf16[16,144,256]{2,1,0:T(8,128)(2,1)S(1)}, u32[]{:S(2)}, u32[]{:S(2)}) async-start(bf16[16,144,256]{2,1,0:T(8,128)(2,1)} %pack.2), calls=%async_computation | async-start | bytes 2359296 | tf_op jit(solution)/shard_map/all_to_all | solution.py:504
  12.7 1.3 collective-permute-start
  14.0 5.5 %pack.3 = bf16[16,144,256]{2,1,0:T(8,128)(2,1)} custom-call(s32[1]{0:T(128)S(6)} %sub.10.half_ref, s32[1,2048]{1,0:T(1,128)} %bitcast.82, s32[1,2048]{1,0:T(1,128)} %bitcast.84, bf16[2048,256]{1,0:T(8,128)(2,1)} %feat_ref.3), custom_call_target="tpu_custom_call" | custom-call | flops 4400000000 | bytes 14000000 | tf_op jit(solution)/shard_map/pack/pallas_call | solution.py:100
  19.6 10.9 %all-to-all-done.refs_2_ = bf16[16,144,256]{2,1,0:T(8,128)(2,1)S(1)} async-done(((bf16[16,144,256]{2,1,0:T(8,128)(2,1)}), bf16[16,144,256]{2,1,0:T(8,128)(2,1)S(1)}, u32[]{:S(2)}, u32[]{:S(2)}) %all-to-all-start) | async-done | bytes 1179680 | tf_op jit(solution)/shard_map/all_to_all | solution.py:504
  30.4 3.7 %all-to-all-start.1 = ((bf16[16,144,256]{2,1,0:T(8,128)(2,1)}), bf16[16,144,256]{2,1,0:T(8,128)(2,1)S(1)}, u32[]{:S(2)}, u32[]{:S(2)}) async-start(bf16[16,144,256]{2,1,0:T(8,128)(2,1)} %pack.3), calls=%async_computation.1 | async-start | bytes 2359296 | tf_op jit(solution)/shard_map/all_to_all | solution.py:504
  34.2 0.6 fusion.12.refs_1_
  34.8 2.6 %collective-permute-start.1 = (bf16[2304,128]{1,0:T(8,128)(2,1)S(1)}, bf16[2304,128]{1,0:T(8,128)(2,1)S(1)}, u32[]{:S(2)}, u32[]{:S(2)}) collective-permute-start(bf16[2304,128]{1,0:T(8,128)(2,1)S(1)} %pad_maximum_fusion.1.refs_5_), channel_id=1, source_target_pairs={{0,16},{16,0},{1,17},{17,1},{2,18},{18,2},{3,19},{19,3},{4,20},{20... | collective-permute-start | bytes 1769480 | tf_op jit(solution)/shard_map/ppermute | solution.py:439
  37.4 30.6 %slab_near.1 = (f32[2048,128]{1,0:T(8,128)}, f32[256,128]{1,0:T(8,128)}, f32[6912,128]{1,0:T(8,128)}, f32[256,256]{1,0:T(8,128)}, f32[1,256]{1,0:T(1,128)}) custom-call(s32[1]{0:T(128)} %bitcast.refs_0_.bit_ref, s32[2048]{0:T(1024)} %fusion.12.refs_1_, bf16[16,144,256]{2,1,0:T(8,128)(2,1)} %copy-done.1, bf16[256,256]{1,0:T(8,128)(2,1)} %refs_3_.5, ...), custom_call_target="tpu_custom_call" | custom-call | flops 28600000512 | bytes 91000000 | tf_op jit(solution)/shard_map/slab_near/pallas_call | solution.py:371
  68.1 0.7 fusion.10.refs_1_
  68.8 0.3 copy-done
  69.1 0.5 copy-done.6
  69.6 20.9 %slab_far_ahead.1 = (bf16[1728,128]{1,0:T(8,128)(2,1)}, bf16[576,128]{1,0:T(8,128)(2,1)}, bf16[3456,128]{1,0:T(8,128)(2,1)}, bf16[3456,128]{1,0:T(8,128)(2,1)}) custom-call(s32[1]{0:T(128)} %bitcast.refs_0_.bit_ref, s32[2048]{0:T(1024)} %fusion.10.refs_1_, bf16[16,144,256]{2,1,0:T(8,128)(2,1)} %copy-done, bf16[256,256]{1,0:T(8,128)(2,1)} %refs_3_.5, ...), custom_call_target="tpu_custom_call" | custom-call | flops 22000001024 | bytes 70000000 | tf_op jit(solution)/shard_map/slab_far_ahead/pallas_call | solution.py:371
  90.6 0.8 collective-permute-start.3
  91.5 1.8 %collective-permute-done.2 = bf16[3456,128]{1,0:T(8,128)(2,1)S(1)} collective-permute-done((bf16[3456,128]{1,0:T(8,128)(2,1)}, bf16[3456,128]{1,0:T(8,128)(2,1)S(1)}, u32[]{:S(2)}, u32[]{:S(2)}) %collective-permute-start.2) | collective-permute-done | bytes 884768 | tf_op jit(solution)/shard_map/ppermute | solution.py:443
  93.2 1.4 add_convert_fusion
  94.7 3.8 %collective-permute-start.4 = (bf16[864,128]{1,0:T(8,128)(2,1)S(1)}, bf16[864,128]{1,0:T(8,128)(2,1)S(1)}, u32[]{:S(2)}, u32[]{:S(2)}) collective-permute-start(bf16[864,128]{1,0:T(8,128)(2,1)S(1)} %get-tuple-element.68), channel_id=1, source_target_pairs={{0,2},{1,3},{2,0},{3,1},{4,6},{5,7},{6,4},{7,5},{8,10},{9,11},{10,... | collective-permute-start | bytes 663560 | tf_op jit(solution)/shard_map/ppermute | solution.py:443
  98.7 1.4 collective-permute-start.6
  100.1 13.4 %slab_far_back.1 = bf16[768,128]{1,0:T(8,128)(2,1)} custom-call(s32[1]{0:T(128)} %bitcast.refs_0_.bit_ref, s32[2048]{0:T(1024)} %fusion.10.refs_1_, bf16[16,144,256]{2,1,0:T(8,128)(2,1)} %copy-done, bf16[256,256]{1,0:T(8,128)(2,1)} %refs_3_.5, f32[1,256]{1,0:T(1,128)} %bitcast.87, bf16[2304,128]{1,0:T(8,128)(2,1)} %copy-done.6, ...), custom_call_target="tpu_custom_call" | custom-call | flops 12099999744 | bytes 38500000 | tf_op jit(solution)/shard_map/slab_far_back/pallas_call | solution.py:371
  113.5 0.3 collective-permute-done.3
  113.8 0.9 dynamic-slice_bitcast_fusion.4
  114.8 0.4 collective-permute-start.11
  115.1 0.9 collective-permute-done.7
  116.0 0.9 fusion.1
  117.0 1.5 collective-permute-start.10
  118.5 3.7 %collective-permute-start.8 = (bf16[96,128]{1,0:T(8,128)(2,1)S(1)}, bf16[96,128]{1,0:T(8,128)(2,1)S(1)}, u32[]{:S(2)}, u32[]{:S(2)}) collective-permute-start(bf16[96,128]{1,0:T(8,128)(2,1)S(1)} %get-tuple-element.77), channel_id=1, source_target_pairs={{0,2},{1,3},{2,0},{3,1},{4,6},{5,7},{6,4},{7,5},{8,10},{9,11},{10,... | collective-permute-start | bytes 73736 | tf_op jit(solution)/shard_map/ppermute | solution.py:443
  122.3 0.1 add_convert_fusion.1
  122.4 1.9 %collective-permute-done.8 = bf16[96,128]{1,0:T(8,128)(2,1)S(1)} collective-permute-done((bf16[96,128]{1,0:T(8,128)(2,1)S(1)}, bf16[96,128]{1,0:T(8,128)(2,1)S(1)}, u32[]{:S(2)}, u32[]{:S(2)}) %collective-permute-start.8) | collective-permute-done | bytes 24608 | tf_op jit(solution)/shard_map/ppermute | solution.py:443
  124.3 1.8 %collective-permute-done.9 = bf16[96,128]{1,0:T(8,128)(2,1)S(1)} collective-permute-done((bf16[96,128]{1,0:T(8,128)(2,1)S(1)}, bf16[96,128]{1,0:T(8,128)(2,1)S(1)}, u32[]{:S(2)}, u32[]{:S(2)}) %collective-permute-start.9) | collective-permute-done | bytes 24608 | tf_op jit(solution)/shard_map/ppermute | solution.py:443
  126.1 0.7 collective-permute-start.12
  126.8 1.2 collective-permute-start.13
  128.0 2.6 %collective-permute-start.14 = (bf16[240,128]{1,0:T(8,128)(2,1)S(1)}, bf16[240,128]{1,0:T(8,128)(2,1)S(1)}, u32[]{:S(2)}, u32[]{:S(2)}) collective-permute-start(bf16[240,128]{1,0:T(8,128)(2,1)S(1)} %get-tuple-element.75), channel_id=1, source_target_pairs={{0,24},{1,25},{2,26},{3,27},{4,28},{5,29},{6,30},{7,31},{8,16},{9,... | collective-permute-start | bytes 184328 | tf_op jit(solution)/shard_map/ppermute | solution.py:443
  130.6 2.4 %collective-permute-done.13 = bf16[240,128]{1,0:T(8,128)(2,1)S(1)} collective-permute-done((bf16[240,128]{1,0:T(8,128)(2,1)S(1)}, bf16[240,128]{1,0:T(8,128)(2,1)S(1)}, u32[]{:S(2)}, u32[]{:S(2)}) %collective-permute-start.13) | collective-permute-done | bytes 61472 | tf_op jit(solution)/shard_map/ppermute | solution.py:443
  133.0 1.1 collective-permute-done.14
  134.2 2.6 %collective-permute-start.15 = (bf16[240,128]{1,0:T(8,128)(2,1)S(1)}, bf16[240,128]{1,0:T(8,128)(2,1)S(1)}, u32[]{:S(2)}, u32[]{:S(2)}) collective-permute-start(bf16[240,128]{1,0:T(8,128)(2,1)S(1)} %fusion.4), channel_id=1, source_target_pairs={{0,24},{1,25},{2,26},{3,27},{4,28},{5,29},{6,30},{7,31},{8,16},{9,... | collective-permute-start | bytes 184328 | tf_op jit(solution)/shard_map/ppermute | solution.py:443
  136.8 1.8 %collective-permute-start.17 = (bf16[240,128]{1,0:T(8,128)(2,1)S(1)}, bf16[240,128]{1,0:T(8,128)(2,1)S(1)}, u32[]{:S(2)}, u32[]{:S(2)}) collective-permute-start(bf16[240,128]{1,0:T(8,128)(2,1)S(1)} %fusion.4), channel_id=1, source_target_pairs={{0,8},{1,9},{2,10},{3,11},{4,12},{5,13},{6,14},{7,15},{8,0},{9,1},... | collective-permute-start | bytes 184328 | tf_op jit(solution)/shard_map/ppermute | solution.py:443
  138.7 1.6 %collective-permute-done.15 = bf16[240,128]{1,0:T(8,128)(2,1)S(1)} collective-permute-done((bf16[240,128]{1,0:T(8,128)(2,1)S(1)}, bf16[240,128]{1,0:T(8,128)(2,1)S(1)}, u32[]{:S(2)}, u32[]{:S(2)}) %collective-permute-start.15) | collective-permute-done | bytes 61472 | tf_op jit(solution)/shard_map/ppermute | solution.py:443
  140.3 1.7 %collective-permute-done.16 = bf16[240,128]{1,0:T(8,128)(2,1)S(1)} collective-permute-done((bf16[240,128]{1,0:T(8,128)(2,1)S(1)}, bf16[240,128]{1,0:T(8,128)(2,1)S(1)}, u32[]{:S(2)}, u32[]{:S(2)}) %collective-permute-start.16) | collective-permute-done | bytes 61472 | tf_op jit(solution)/shard_map/ppermute | solution.py:443
  142.0 1.6 collective-permute-start.18
  143.6 2.4 %collective-permute-start.19 = (bf16[960,128]{1,0:T(8,128)(2,1)S(1)}, bf16[960,128]{1,0:T(8,128)(2,1)S(1)}, u32[]{:S(2)}, u32[]{:S(2)}) collective-permute-start(bf16[960,128]{1,0:T(8,128)(2,1)S(1)} %pad_maximum_fusion.4), channel_id=1, source_target_pairs={{0,4},{1,5},{2,6},{3,7},{4,0},{5,1},{6,2},{7,3},{8,12},{9,13},{10,... | collective-permute-start | bytes 737288 | tf_op jit(solution)/shard_map/ppermute | solution.py:443
  146.0 1.3 collective-permute-start.21
  147.4 3.8 %collective-permute-done.18 = bf16[960,128]{1,0:T(8,128)(2,1)S(1)} collective-permute-done((bf16[960,128]{1,0:T(8,128)(2,1)S(1)}, bf16[960,128]{1,0:T(8,128)(2,1)S(1)}, u32[]{:S(2)}, u32[]{:S(2)}) %collective-permute-start.18) | collective-permute-done | bytes 245792 | tf_op jit(solution)/shard_map/ppermute | solution.py:443
  151.1 2.9 %collective-permute-done.19 = bf16[960,128]{1,0:T(8,128)(2,1)S(1)} collective-permute-done((bf16[960,128]{1,0:T(8,128)(2,1)S(1)}, bf16[960,128]{1,0:T(8,128)(2,1)S(1)}, u32[]{:S(2)}, u32[]{:S(2)}) %collective-permute-start.19) | collective-permute-done | bytes 245792 | tf_op jit(solution)/shard_map/ppermute | solution.py:443
  154.0 1.2 collective-permute-done.20
  155.5 1.1 copy-done.2
  156.7 0.1 fusion
  157.0 1.1 pad_maximum_fusion.2
  158.1 2.2 %finish.1 = (f32[6912,128]{1,0:T(8,128)}, f32[256,256]{1,0:T(8,128)}, f32[1,256]{1,0:T(1,128)}) custom-call(s32[1]{0:T(128)} %bitcast.refs_0_.bit_ref, bf16[3840,128]{1,0:T(8,128)(2,1)S(1)} %pad_maximum_fusion.mine_ref, bf16[3840,128]{1,0:T(8,128)(2,1)S(1)} %collective-permute-done.22.theirs_ref), custom_call_target="tpu_custom_call" | custom-call | flops 3300000000 | bytes 10500000 | tf_op jit(solution)/shard_map/finish/pallas_call | solution.py:409
  (55 shorter events, 1.3 us)
Async XLA Ops:
  6.1 6.4 %copy-start.3 = (bf16[1,16,16,8,128]{4,3,2,1,0:T(8,128)(2,1)S(1)}, bf16[1,16,16,8,128]{4,3,2,1,0:T(8,128)(2,1)}, u32[]{:S(2)}) copy-start(bf16[1,16,16,8,128]{4,3,2,1,0:T(8,128)(2,1)} %param.13) | copy-start | bytes 1572868
  6.1 24.3 %all-to-all-start = ((bf16[16,144,256]{2,1,0:T(8,128)(2,1)}), bf16[16,144,256]{2,1,0:T(8,128)(2,1)S(1)}, u32[]{:S(2)}, u32[]{:S(2)}) async-start(bf16[16,144,256]{2,1,0:T(8,128)(2,1)} %pack.2), calls=%async_computation | async-start | bytes 2359296 | tf_op jit(solution)/shard_map/all_to_all | solution.py:504
  12.7 6.8 %collective-permute-start = (bf16[256,128]{1,0:T(8,128)(2,1)S(1)}, bf16[256,128]{1,0:T(8,128)(2,1)S(1)}, u32[]{:S(2)}, u32[]{:S(2)}) collective-permute-start(bf16[256,128]{1,0:T(8,128)(2,1)S(1)} %bitcast.76), channel_id=1, source_target_pairs={{1,0},{2,1},{3,2},{5,4},{6,5},{7,6},{9,8},{10,9},{11,10},{13,12},{... | collective-permute-start | bytes 196616 | tf_op jit(solution)/shard_map/ppermute | solution.py:435
  19.5 15.3 %copy-start.4 = (bf16[2304,128]{1,0:T(8,128)(2,1)}, bf16[2304,128]{1,0:T(8,128)(2,1)S(1)}, u32[]{:S(2)}) copy-start(bf16[2304,128]{1,0:T(8,128)(2,1)S(1)} %pad_maximum_fusion.1.refs_5_) | copy-start | bytes 1769476
  30.4 3.7 %copy-start.1 = (bf16[16,144,256]{2,1,0:T(8,128)(2,1)}, bf16[16,144,256]{2,1,0:T(8,128)(2,1)S(1)}, u32[]{:S(2)}) copy-start(bf16[16,144,256]{2,1,0:T(8,128)(2,1)S(1)} %all-to-all-done.refs_2_) | copy-start | bytes 3538948
  30.4 37.6 %all-to-all-start.1 = ((bf16[16,144,256]{2,1,0:T(8,128)(2,1)}), bf16[16,144,256]{2,1,0:T(8,128)(2,1)S(1)}, u32[]{:S(2)}, u32[]{:S(2)}) async-start(bf16[16,144,256]{2,1,0:T(8,128)(2,1)} %pack.3), calls=%async_computation.1 | async-start | bytes 2359296 | tf_op jit(solution)/shard_map/all_to_all | solution.py:504
  34.8 34.0 %collective-permute-start.1 = (bf16[2304,128]{1,0:T(8,128)(2,1)S(1)}, bf16[2304,128]{1,0:T(8,128)(2,1)S(1)}, u32[]{:S(2)}, u32[]{:S(2)}) collective-permute-start(bf16[2304,128]{1,0:T(8,128)(2,1)S(1)} %pad_maximum_fusion.1.refs_5_), channel_id=1, source_target_pairs={{0,16},{16,0},{1,17},{17,1},{2,18},{18,2},{3,19},{19,3},{4,20},{20... | collective-permute-start | bytes 1769480 | tf_op jit(solution)/shard_map/ppermute | solution.py:439
  68.0 1.0 copy-start
  68.8 0.8 copy-start.6
  90.5 2.7 %collective-permute-start.2 = (bf16[3456,128]{1,0:T(8,128)(2,1)}, bf16[3456,128]{1,0:T(8,128)(2,1)S(1)}, u32[]{:S(2)}, u32[]{:S(2)}) collective-permute-start(bf16[3456,128]{1,0:T(8,128)(2,1)} %get-tuple-element.38), channel_id=1, source_target_pairs={{0,1},{1,0},{2,3},{3,2},{4,5},{5,4},{6,7},{7,6},{8,9},{9,8},{10,11... | collective-permute-start | bytes 2654216 | tf_op jit(solution)/shard_map/ppermute | solution.py:443
  90.6 23.2 %collective-permute-start.3 = (bf16[1728,128]{1,0:T(8,128)(2,1)}, bf16[1728,128]{1,0:T(8,128)(2,1)S(1)}, u32[]{:S(2)}, u32[]{:S(2)}) collective-permute-start(bf16[1728,128]{1,0:T(8,128)(2,1)} %get-tuple-element.42), channel_id=1, source_target_pairs={{0,16},{16,0},{1,17},{17,1},{2,18},{18,2},{3,19},{19,3},{4,20},{20... | collective-permute-start | bytes 1327112 | tf_op jit(solution)/shard_map/ppermute | solution.py:439
  94.7 19.1 %collective-permute-start.4 = (bf16[864,128]{1,0:T(8,128)(2,1)S(1)}, bf16[864,128]{1,0:T(8,128)(2,1)S(1)}, u32[]{:S(2)}, u32[]{:S(2)}) collective-permute-start(bf16[864,128]{1,0:T(8,128)(2,1)S(1)} %get-tuple-element.68), channel_id=1, source_target_pairs={{0,2},{1,3},{2,0},{3,1},{4,6},{5,7},{6,4},{7,5},{8,10},{9,11},{10,... | collective-permute-start | bytes 663560 | tf_op jit(solution)/shard_map/ppermute | solution.py:443
  98.5 15.3 %collective-permute-start.5 = (bf16[864,128]{1,0:T(8,128)(2,1)S(1)}, bf16[864,128]{1,0:T(8,128)(2,1)S(1)}, u32[]{:S(2)}, u32[]{:S(2)}) collective-permute-start(bf16[864,128]{1,0:T(8,128)(2,1)S(1)} %get-tuple-element.67), channel_id=1, source_target_pairs={{0,4},{1,5},{2,6},{3,7},{4,0},{5,1},{6,2},{7,3},{8,12},{9,13},{10,... | collective-permute-start | bytes 663560 | tf_op jit(solution)/shard_map/ppermute | solution.py:443
  98.7 15.1 %collective-permute-start.6 = (bf16[864,128]{1,0:T(8,128)(2,1)S(1)}, bf16[864,128]{1,0:T(8,128)(2,1)S(1)}, u32[]{:S(2)}, u32[]{:S(2)}) collective-permute-start(bf16[864,128]{1,0:T(8,128)(2,1)S(1)} %get-tuple-element.66), channel_id=1, source_target_pairs={{0,6},{1,7},{2,4},{3,5},{4,2},{5,3},{6,0},{7,1},{8,14},{9,15},{10,... | collective-permute-start | bytes 663560 | tf_op jit(solution)/shard_map/ppermute | solution.py:443
  100.1 14.7 %copy-start.7 = (bf16[576,128]{1,0:T(8,128)(2,1)S(1)}, bf16[576,128]{1,0:T(8,128)(2,1)}, u32[]{:S(2)}) copy-start(bf16[576,128]{1,0:T(8,128)(2,1)} %get-tuple-element.50) | copy-start | bytes 442372
  114.7 1.3 collective-permute-start.7
  114.8 11.3 %collective-permute-start.11 = (bf16[576,128]{1,0:T(8,128)(2,1)S(1)}, bf16[576,128]{1,0:T(8,128)(2,1)S(1)}, u32[]{:S(2)}, u32[]{:S(2)}) collective-permute-start(bf16[576,128]{1,0:T(8,128)(2,1)S(1)} %copy-done.7), channel_id=1, source_target_pairs={{0,16},{16,0},{1,17},{17,1},{2,18},{18,2},{3,19},{19,3},{4,20},{20... | collective-permute-start | bytes 442376 | tf_op jit(solution)/shard_map/ppermute | solution.py:439
  117.0 5.4 %collective-permute-start.10 = (bf16[96,128]{1,0:T(8,128)(2,1)S(1)}, bf16[96,128]{1,0:T(8,128)(2,1)S(1)}, u32[]{:S(2)}, u32[]{:S(2)}) collective-permute-start(bf16[96,128]{1,0:T(8,128)(2,1)S(1)} %get-tuple-element.78), channel_id=1, source_target_pairs={{0,6},{1,7},{2,4},{3,5},{4,2},{5,3},{6,0},{7,1},{8,14},{9,15},{10,... | collective-permute-start | bytes 73736 | tf_op jit(solution)/shard_map/ppermute | solution.py:443
  118.5 5.8 %collective-permute-start.8 = (bf16[96,128]{1,0:T(8,128)(2,1)S(1)}, bf16[96,128]{1,0:T(8,128)(2,1)S(1)}, u32[]{:S(2)}, u32[]{:S(2)}) collective-permute-start(bf16[96,128]{1,0:T(8,128)(2,1)S(1)} %get-tuple-element.77), channel_id=1, source_target_pairs={{0,2},{1,3},{2,0},{3,1},{4,6},{5,7},{6,4},{7,5},{8,10},{9,11},{10,... | collective-permute-start | bytes 73736 | tf_op jit(solution)/shard_map/ppermute | solution.py:443
  122.2 16.4 %copy-start.5 = (f32[256,128]{1,0:T(8,128)S(1)}, f32[256,128]{1,0:T(8,128)}, u32[]{:S(2)}) copy-start(f32[256,128]{1,0:T(8,128)} %get-tuple-element.54) | copy-start | bytes 393220
  122.2 3.8 %collective-permute-start.9 = (bf16[96,128]{1,0:T(8,128)(2,1)S(1)}, bf16[96,128]{1,0:T(8,128)(2,1)S(1)}, u32[]{:S(2)}, u32[]{:S(2)}) collective-permute-start(bf16[96,128]{1,0:T(8,128)(2,1)S(1)} %get-tuple-element.79), channel_id=1, source_target_pairs={{0,4},{1,5},{2,6},{3,7},{4,0},{5,1},{6,2},{7,3},{8,12},{9,13},{10,... | collective-permute-start | bytes 73736 | tf_op jit(solution)/shard_map/ppermute | solution.py:443
  126.1 4.5 %collective-permute-start.12 = (bf16[240,128]{1,0:T(8,128)(2,1)S(1)}, bf16[240,128]{1,0:T(8,128)(2,1)S(1)}, u32[]{:S(2)}, u32[]{:S(2)}) collective-permute-start(bf16[240,128]{1,0:T(8,128)(2,1)S(1)} %get-tuple-element.74), channel_id=1, source_target_pairs={{0,8},{1,9},{2,10},{3,11},{4,12},{5,13},{6,14},{7,15},{8,0},{9,1},... | collective-permute-start | bytes 184328 | tf_op jit(solution)/shard_map/ppermute | solution.py:443
  126.8 6.2 %collective-permute-start.13 = (bf16[240,128]{1,0:T(8,128)(2,1)S(1)}, bf16[240,128]{1,0:T(8,128)(2,1)S(1)}, u32[]{:S(2)}, u32[]{:S(2)}) collective-permute-start(bf16[240,128]{1,0:T(8,128)(2,1)S(1)} %get-tuple-element.76), channel_id=1, source_target_pairs={{0,16},{1,17},{2,18},{3,19},{4,20},{5,21},{6,22},{7,23},{8,24},{9,... | collective-permute-start | bytes 184328 | tf_op jit(solution)/shard_map/ppermute | solution.py:443
  128.0 6.1 %collective-permute-start.14 = (bf16[240,128]{1,0:T(8,128)(2,1)S(1)}, bf16[240,128]{1,0:T(8,128)(2,1)S(1)}, u32[]{:S(2)}, u32[]{:S(2)}) collective-permute-start(bf16[240,128]{1,0:T(8,128)(2,1)S(1)} %get-tuple-element.75), channel_id=1, source_target_pairs={{0,24},{1,25},{2,26},{3,27},{4,28},{5,29},{6,30},{7,31},{8,16},{9,... | collective-permute-start | bytes 184328 | tf_op jit(solution)/shard_map/ppermute | solution.py:443
  134.2 6.1 %collective-permute-start.15 = (bf16[240,128]{1,0:T(8,128)(2,1)S(1)}, bf16[240,128]{1,0:T(8,128)(2,1)S(1)}, u32[]{:S(2)}, u32[]{:S(2)}) collective-permute-start(bf16[240,128]{1,0:T(8,128)(2,1)S(1)} %fusion.4), channel_id=1, source_target_pairs={{0,24},{1,25},{2,26},{3,27},{4,28},{5,29},{6,30},{7,31},{8,16},{9,... | collective-permute-start | bytes 184328 | tf_op jit(solution)/shard_map/ppermute | solution.py:443
  136.8 5.1 %collective-permute-start.16 = (bf16[240,128]{1,0:T(8,128)(2,1)S(1)}, bf16[240,128]{1,0:T(8,128)(2,1)S(1)}, u32[]{:S(2)}, u32[]{:S(2)}) collective-permute-start(bf16[240,128]{1,0:T(8,128)(2,1)S(1)} %fusion.4), channel_id=1, source_target_pairs={{0,16},{1,17},{2,18},{3,19},{4,20},{5,21},{6,22},{7,23},{8,24},{9,... | collective-permute-start | bytes 184328 | tf_op jit(solution)/shard_map/ppermute | solution.py:443
  136.8 5.1 %collective-permute-start.17 = (bf16[240,128]{1,0:T(8,128)(2,1)S(1)}, bf16[240,128]{1,0:T(8,128)(2,1)S(1)}, u32[]{:S(2)}, u32[]{:S(2)}) collective-permute-start(bf16[240,128]{1,0:T(8,128)(2,1)S(1)} %fusion.4), channel_id=1, source_target_pairs={{0,8},{1,9},{2,10},{3,11},{4,12},{5,13},{6,14},{7,15},{8,0},{9,1},... | collective-permute-start | bytes 184328 | tf_op jit(solution)/shard_map/ppermute | solution.py:443
  142.0 9.1 %collective-permute-start.18 = (bf16[960,128]{1,0:T(8,128)(2,1)S(1)}, bf16[960,128]{1,0:T(8,128)(2,1)S(1)}, u32[]{:S(2)}, u32[]{:S(2)}) collective-permute-start(bf16[960,128]{1,0:T(8,128)(2,1)S(1)} %pad_maximum_fusion.4), channel_id=1, source_target_pairs={{0,6},{1,7},{2,4},{3,5},{4,2},{5,3},{6,0},{7,1},{8,14},{9,15},{10,... | collective-permute-start | bytes 737288 | tf_op jit(solution)/shard_map/ppermute | solution.py:443
  143.6 10.4 %collective-permute-start.19 = (bf16[960,128]{1,0:T(8,128)(2,1)S(1)}, bf16[960,128]{1,0:T(8,128)(2,1)S(1)}, u32[]{:S(2)}, u32[]{:S(2)}) collective-permute-start(bf16[960,128]{1,0:T(8,128)(2,1)S(1)} %pad_maximum_fusion.4), channel_id=1, source_target_pairs={{0,4},{1,5},{2,6},{3,7},{4,0},{5,1},{6,2},{7,3},{8,12},{9,13},{10,... | collective-permute-start | bytes 737288 | tf_op jit(solution)/shard_map/ppermute | solution.py:443
  146.0 9.2 %collective-permute-start.20 = (bf16[960,128]{1,0:T(8,128)(2,1)S(1)}, bf16[960,128]{1,0:T(8,128)(2,1)S(1)}, u32[]{:S(2)}, u32[]{:S(2)}) collective-permute-start(bf16[960,128]{1,0:T(8,128)(2,1)S(1)} %pad_maximum_fusion.4), channel_id=1, source_target_pairs={{0,2},{1,3},{2,0},{3,1},{4,6},{5,7},{6,4},{7,5},{8,10},{9,11},{10,... | collective-permute-start | bytes 737288 | tf_op jit(solution)/shard_map/ppermute | solution.py:443
  146.0 9.3 %collective-permute-start.21 = (f32[256,128]{1,0:T(8,128)S(1)}, f32[256,128]{1,0:T(8,128)S(1)}, u32[]{:S(2)}, u32[]{:S(2)}) collective-permute-start(f32[256,128]{1,0:T(8,128)S(1)} %convert_add_fusion.1), channel_id=1, source_target_pairs={{0,1},{1,2},{2,3},{4,5},{5,6},{6,7},{8,9},{9,10},{10,11},{12,13},{... | collective-permute-start | bytes 393224 | tf_op jit(solution)/shard_map/ppermute | solution.py:435
  155.3 1.2 copy-start.2
  155.4 2.7 %collective-permute-start.22 = (bf16[3840,128]{1,0:T(8,128)(2,1)S(1)}, bf16[3840,128]{1,0:T(8,128)(2,1)S(1)}, u32[]{:S(2)}, u32[]{:S(2)}) collective-permute-start(bf16[3840,128]{1,0:T(8,128)(2,1)S(1)} %pad_maximum_fusion.mine_ref), channel_id=1, source_target_pairs={{0,1},{1,0},{2,3},{3,2},{4,5},{5,4},{6,7},{7,6},{8,9},{9,8},{10,11... | collective-permute-start | bytes 2949128 | tf_op jit(solution)/shard_map/ppermute | solution.py:443
where the time goes:
time: 161 us; the launch traced here: 160 us
  Pallas kernels  78.1 us (49%)
  starting transfers between devices  40.2 us (25%)
  waiting for transfers between devices  32.2 us (20%)
  other arithmetic  5.38 us (3%)
  local copies, waits for them, and re-layouts  3.32 us (2%)
    pallas_call x3, Pallas kernels, slab(): pl.pallas_call(functools.partial(slab_kernel, cap, scale, dims, kind), ou...  64.9 us
    ppermute x18, starting transfers between devices, exchange(): lax.ppermute(array, AXES, [(i, i ^ mask) for i in range(lax.axis_size(AXE...  23.7 us
    ppermute x18, waiting for transfers between devices, exchange(): lax.ppermute(array, AXES, [(i, i ^ mask) for i in range(lax.axis_size(AXE...  21 us
    pallas_call x2, Pallas kernels, pack(): pl.pallas_call(functools.partial(pack_kernel, group, cap, dims), out_shap...  11 us
    all_to_all x2, waiting for transfers between devices, swapped(): lax.all_to_all(packed, ('dom', 'brick'), split_axis=0, concat_axis=0, til...  10.9 us
    all_to_all x2, starting transfers between devices, swapped(): lax.all_to_all(packed, ('dom', 'brick'), split_axis=0, concat_axis=0, til...  10.1 us
    ppermute x3, starting transfers between devices, crossed(): return lax.ppermute(array, 'half', [(0, 1), (1, 0)])  3.8 us
  transfers between devices with their start and end apart: 25, of which 13 were waited for; matrix products, arithmetic and copies ran while one was open for 4% of the time, Pallas kernels for 31%

commit v1 on v0

--- a/solution.py
+++ b/solution.py
@@ -155,7 +155,7 @@
 
 
 UNROLL = 16
-CHUNK = 512
+CHUNK = 1024
 
 
 def pairs_of(ref):
@@ -353,7 +353,7 @@
         scratch += [slopes, wide, tall, terms] + outputs
     elif kind == "far_ahead":
         in_specs += [ANY]
-        lent = (cells + cells // half_z) * 3 // 4
+        lent = (cells + cells // half_z) * 11 // 16
         out_shape = (
             jax.ShapeDtypeStruct((lent, out_width), BF16),
             jax.ShapeDtypeStruct((cells + cells // half_z - lent, out_width), BF16),

time: 161 us -> 160 us (level)
  waiting for transfers between devices: 32.2 us -> 34.5 us
  starting transfers between devices: 40.2 us -> 38.3 us
    ppermute x3, waiting for transfers between devices: 0.34 us -> 2.79 us  [crossed(): return lax.ppermute(array, 'half', [(0, 1), (1, 0)])]
  transfers between devices with their start and end apart: 25 -> 25, of which waited for: 13 -> 14; matrix products, arithmetic and copies ran while one was open for 4% -> 4% of each run, Pallas kernels for 31% -> 29%
where the time goes in v1:
time: 160 us; the launch traced here: 159 us
  Pallas kernels  76.6 us (48%)
  starting transfers between devices  38.3 us (24%)
  waiting for transfers between devices  34.5 us (22%)
  other arithmetic  5.43 us (3%)
  local copies, waits for them, and re-layouts  3.32 us (2%)
    pallas_call x3, Pallas kernels, slab(): pl.pallas_call(functools.partial(slab_kernel, cap, scale, dims, kind), ou...  63.3 us
    ppermute x18, starting transfers between devices, exchange(): lax.ppermute(array, AXES, [(i, i ^ mask) for i in range(lax.axis_size(AXE...  22.3 us
    ppermute x18, waiting for transfers between devices, exchange(): lax.ppermute(array, AXES, [(i, i ^ mask) for i in range(lax.axis_size(AXE...  20.8 us
    pallas_call x2, Pallas kernels, pack(): pl.pallas_call(functools.partial(pack_kernel, group, cap, dims), out_shap...  11 us
    all_to_all x2, waiting for transfers between devices, swapped(): lax.all_to_all(packed, ('dom', 'brick'), split_axis=0, concat_axis=0, til...  10.9 us
    all_to_all x2, starting transfers between devices, swapped(): lax.all_to_all(packed, ('dom', 'brick'), split_axis=0, concat_axis=0, til...  10.1 us
    ppermute x3, starting transfers between devices, crossed(): return lax.ppermute(array, 'half', [(0, 1), (1, 0)])  3.23 us
  transfers between devices with their start and end apart: 25, of which 14 were waited for; matrix products, arithmetic and copies ran while one was open for 4% of the time, Pallas kernels for 29%

profile of v1, /device:TPU:0, one launch (start us, length us, event | category | flops | bytes accessed | tf_op | source)
XLA Modules:
  0.0 159.1 jit_solution(6207031127030397331)
XLA Ops:
  0.6 5.5 %pack.2 = bf16[16,144,256]{2,1,0:T(8,128)(2,1)} custom-call(s32[1]{0:T(128)} %bitcast.3.half_ref, s32[1,2048]{1,0:T(1,128)} %bitcast.81, s32[1,2048]{1,0:T(1,128)} %bitcast.83, bf16[2048,256]{1,0:T(8,128)(2,1)} %feat_ref.3), custom_call_target="tpu_custom_call" | custom-call | flops 4400000000 | bytes 14000000 | tf_op jit(solution)/shard_map/pack/pallas_call | solution.py:100
  6.1 6.4 %all-to-all-start = ((bf16[16,144,256]{2,1,0:T(8,128)(2,1)}), bf16[16,144,256]{2,1,0:T(8,128)(2,1)S(1)}, u32[]{:S(2)}, u32[]{:S(2)}) async-start(bf16[16,144,256]{2,1,0:T(8,128)(2,1)} %pack.2), calls=%async_computation | async-start | bytes 2359296 | tf_op jit(solution)/shard_map/all_to_all | solution.py:504
  12.7 1.3 collective-permute-start
  14.0 5.5 %pack.3 = bf16[16,144,256]{2,1,0:T(8,128)(2,1)} custom-call(s32[1]{0:T(128)S(6)} %sub.10.half_ref, s32[1,2048]{1,0:T(1,128)} %bitcast.82, s32[1,2048]{1,0:T(1,128)} %bitcast.84, bf16[2048,256]{1,0:T(8,128)(2,1)} %feat_ref.3), custom_call_target="tpu_custom_call" | custom-call | flops 4400000000 | bytes 14000000 | tf_op jit(solution)/shard_map/pack/pallas_call | solution.py:100
  19.6 10.9 %all-to-all-done.refs_2_ = bf16[16,144,256]{2,1,0:T(8,128)(2,1)S(1)} async-done(((bf16[16,144,256]{2,1,0:T(8,128)(2,1)}), bf16[16,144,256]{2,1,0:T(8,128)(2,1)S(1)}, u32[]{:S(2)}, u32[]{:S(2)}) %all-to-all-start) | async-done | bytes 1179680 | tf_op jit(solution)/shard_map/all_to_all | solution.py:504
  30.4 3.7 %all-to-all-start.1 = ((bf16[16,144,256]{2,1,0:T(8,128)(2,1)}), bf16[16,144,256]{2,1,0:T(8,128)(2,1)S(1)}, u32[]{:S(2)}, u32[]{:S(2)}) async-start(bf16[16,144,256]{2,1,0:T(8,128)(2,1)} %pack.3), calls=%async_computation.1 | async-start | bytes 2359296 | tf_op jit(solution)/shard_map/all_to_all | solution.py:504
  34.2 0.6 fusion.12.refs_1_
  34.8 2.6 %collective-permute-start.1 = (bf16[2304,128]{1,0:T(8,128)(2,1)S(1)}, bf16[2304,128]{1,0:T(8,128)(2,1)S(1)}, u32[]{:S(2)}, u32[]{:S(2)}) collective-permute-start(bf16[2304,128]{1,0:T(8,128)(2,1)S(1)} %pad_maximum_fusion.1.refs_5_), channel_id=1, source_target_pairs={{0,16},{16,0},{1,17},{17,1},{2,18},{18,2},{3,19},{19,3},{4,20},{20... | collective-permute-start | bytes 1769480 | tf_op jit(solution)/shard_map/ppermute | solution.py:439
  37.4 28.1 %slab_near.1 = (f32[2048,128]{1,0:T(8,128)}, f32[256,128]{1,0:T(8,128)}, f32[6912,128]{1,0:T(8,128)}, f32[256,256]{1,0:T(8,128)}, f32[1,256]{1,0:T(1,128)}) custom-call(s32[1]{0:T(128)} %bitcast.refs_0_.bit_ref, s32[2048]{0:T(1024)} %fusion.12.refs_1_, bf16[16,144,256]{2,1,0:T(8,128)(2,1)} %copy-done.1, bf16[256,256]{1,0:T(8,128)(2,1)} %refs_3_.5, ...), custom_call_target="tpu_custom_call" | custom-call | flops 28600000512 | bytes 91000000 | tf_op jit(solution)/shard_map/slab_near/pallas_call | solution.py:371
  65.6 0.7 fusion.10.refs_1_
  66.3 0.3 copy-done
  66.6 0.5 copy-done.6
  67.1 22.7 %slab_far_ahead.1 = (bf16[1584,128]{1,0:T(8,128)(2,1)}, bf16[720,128]{1,0:T(8,128)(2,1)}, bf16[3456,128]{1,0:T(8,128)(2,1)}, bf16[3456,128]{1,0:T(8,128)(2,1)}) custom-call(s32[1]{0:T(128)} %bitcast.refs_0_.bit_ref, s32[2048]{0:T(1024)} %fusion.10.refs_1_, bf16[16,144,256]{2,1,0:T(8,128)(2,1)} %copy-done, bf16[256,256]{1,0:T(8,128)(2,1)} %refs_3_.5, ...), custom_call_target="tpu_custom_call" | custom-call | flops 22000001024 | bytes 70000000 | tf_op jit(solution)/shard_map/slab_far_ahead/pallas_call | solution.py:371
  89.7 1.3 collective-permute-start.2
  91.1 0.6 collective-permute-start.3
  91.6 1.7 %collective-permute-done.2 = bf16[3456,128]{1,0:T(8,128)(2,1)S(1)} collective-permute-done((bf16[3456,128]{1,0:T(8,128)(2,1)}, bf16[3456,128]{1,0:T(8,128)(2,1)S(1)}, u32[]{:S(2)}, u32[]{:S(2)}) %collective-permute-start.2) | collective-permute-done | bytes 884768 | tf_op jit(solution)/shard_map/ppermute | solution.py:443
  93.3 1.4 add_convert_fusion
  94.8 2.7 %collective-permute-start.4 = (bf16[864,128]{1,0:T(8,128)(2,1)S(1)}, bf16[864,128]{1,0:T(8,128)(2,1)S(1)}, u32[]{:S(2)}, u32[]{:S(2)}) collective-permute-start(bf16[864,128]{1,0:T(8,128)(2,1)S(1)} %get-tuple-element.68), channel_id=1, source_target_pairs={{0,2},{1,3},{2,0},{3,1},{4,6},{5,7},{6,4},{7,5},{8,10},{9,11},{10,... | collective-permute-start | bytes 663560 | tf_op jit(solution)/shard_map/ppermute | solution.py:443
  97.5 1.3 collective-permute-start.5
  98.8 0.3 collective-permute-start.6
  99.2 12.6 %slab_far_back.1 = bf16[768,128]{1,0:T(8,128)(2,1)} custom-call(s32[1]{0:T(128)} %bitcast.refs_0_.bit_ref, s32[2048]{0:T(1024)} %fusion.10.refs_1_, bf16[16,144,256]{2,1,0:T(8,128)(2,1)} %copy-done, bf16[256,256]{1,0:T(8,128)(2,1)} %refs_3_.5, f32[1,256]{1,0:T(1,128)} %bitcast.87, bf16[2304,128]{1,0:T(8,128)(2,1)} %copy-done.6, ...), custom_call_target="tpu_custom_call" | custom-call | flops 12099999744 | bytes 38500000 | tf_op jit(solution)/shard_map/slab_far_back/pallas_call | solution.py:371
  111.7 0.5 collective-permute-done.3
  112.3 0.9 dynamic-slice_bitcast_fusion.4
  113.3 1.2 collective-permute-done.7
  114.5 0.9 fusion.1
  115.4 3.3 %collective-permute-start.10 = (bf16[96,128]{1,0:T(8,128)(2,1)S(1)}, bf16[96,128]{1,0:T(8,128)(2,1)S(1)}, u32[]{:S(2)}, u32[]{:S(2)}) collective-permute-start(bf16[96,128]{1,0:T(8,128)(2,1)S(1)} %get-tuple-element.78), channel_id=1, source_target_pairs={{0,6},{1,7},{2,4},{3,5},{4,2},{5,3},{6,0},{7,1},{8,14},{9,15},{10,... | collective-permute-start | bytes 73736 | tf_op jit(solution)/shard_map/ppermute | solution.py:443
  118.7 0.2 collective-permute-start.8
  119.0 0.7 collective-permute-start.9
  119.8 0.8 collective-permute-done.10
  120.5 2.0 %collective-permute-done.8 = bf16[96,128]{1,0:T(8,128)(2,1)S(1)} collective-permute-done((bf16[96,128]{1,0:T(8,128)(2,1)S(1)}, bf16[96,128]{1,0:T(8,128)(2,1)S(1)}, u32[]{:S(2)}, u32[]{:S(2)}) %collective-permute-start.8) | collective-permute-done | bytes 24608 | tf_op jit(solution)/shard_map/ppermute | solution.py:443
  122.6 0.2 collective-permute-done.9
  122.8 2.3 %collective-permute-done.11 = bf16[720,128]{1,0:T(8,128)(2,1)S(1)} collective-permute-done((bf16[720,128]{1,0:T(8,128)(2,1)S(1)}, bf16[720,128]{1,0:T(8,128)(2,1)S(1)}, u32[]{:S(2)}, u32[]{:S(2)}) %collective-permute-start.11) | collective-permute-done | bytes 184352 | tf_op jit(solution)/shard_map/ppermute | solution.py:439
  125.2 1.7 %collective-permute-start.13 = (bf16[240,128]{1,0:T(8,128)(2,1)S(1)}, bf16[240,128]{1,0:T(8,128)(2,1)S(1)}, u32[]{:S(2)}, u32[]{:S(2)}) collective-permute-start(bf16[240,128]{1,0:T(8,128)(2,1)S(1)} %get-tuple-element.76), channel_id=1, source_target_pairs={{0,16},{1,17},{2,18},{3,19},{4,20},{5,21},{6,22},{7,23},{8,24},{9,... | collective-permute-start | bytes 184328 | tf_op jit(solution)/shard_map/ppermute | solution.py:443
  126.9 2.7 %collective-permute-start.14 = (bf16[240,128]{1,0:T(8,128)(2,1)S(1)}, bf16[240,128]{1,0:T(8,128)(2,1)S(1)}, u32[]{:S(2)}, u32[]{:S(2)}) collective-permute-start(bf16[240,128]{1,0:T(8,128)(2,1)S(1)} %get-tuple-element.75), channel_id=1, source_target_pairs={{0,24},{1,25},{2,26},{3,27},{4,28},{5,29},{6,30},{7,31},{8,16},{9,... | collective-permute-start | bytes 184328 | tf_op jit(solution)/shard_map/ppermute | solution.py:443
  129.7 3.3 %collective-permute-done.13 = bf16[240,128]{1,0:T(8,128)(2,1)S(1)} collective-permute-done((bf16[240,128]{1,0:T(8,128)(2,1)S(1)}, bf16[240,128]{1,0:T(8,128)(2,1)S(1)}, u32[]{:S(2)}, u32[]{:S(2)}) %collective-permute-start.13) | collective-permute-done | bytes 61472 | tf_op jit(solution)/shard_map/ppermute | solution.py:443
  133.1 2.7 %collective-permute-start.15 = (bf16[240,128]{1,0:T(8,128)(2,1)S(1)}, bf16[240,128]{1,0:T(8,128)(2,1)S(1)}, u32[]{:S(2)}, u32[]{:S(2)}) collective-permute-start(bf16[240,128]{1,0:T(8,128)(2,1)S(1)} %fusion.4), channel_id=1, source_target_pairs={{0,24},{1,25},{2,26},{3,27},{4,28},{5,29},{6,30},{7,31},{8,16},{9,... | collective-permute-start | bytes 184328 | tf_op jit(solution)/shard_map/ppermute | solution.py:443
  135.8 1.7 %collective-permute-start.17 = (bf16[240,128]{1,0:T(8,128)(2,1)S(1)}, bf16[240,128]{1,0:T(8,128)(2,1)S(1)}, u32[]{:S(2)}, u32[]{:S(2)}) collective-permute-start(bf16[240,128]{1,0:T(8,128)(2,1)S(1)} %fusion.4), channel_id=1, source_target_pairs={{0,8},{1,9},{2,10},{3,11},{4,12},{5,13},{6,14},{7,15},{8,0},{9,1},... | collective-permute-start | bytes 184328 | tf_op jit(solution)/shard_map/ppermute | solution.py:443
  137.5 1.8 %collective-permute-done.15 = bf16[240,128]{1,0:T(8,128)(2,1)S(1)} collective-permute-done((bf16[240,128]{1,0:T(8,128)(2,1)S(1)}, bf16[240,128]{1,0:T(8,128)(2,1)S(1)}, u32[]{:S(2)}, u32[]{:S(2)}) %collective-permute-start.15) | collective-permute-done | bytes 61472 | tf_op jit(solution)/shard_map/ppermute | solution.py:443
  139.4 1.5 collective-permute-done.16
  141.0 2.3 %collective-permute-start.18 = (bf16[960,128]{1,0:T(8,128)(2,1)S(1)}, bf16[960,128]{1,0:T(8,128)(2,1)S(1)}, u32[]{:S(2)}, u32[]{:S(2)}) collective-permute-start(bf16[960,128]{1,0:T(8,128)(2,1)S(1)} %pad_maximum_fusion.4), channel_id=1, source_target_pairs={{0,6},{1,7},{2,4},{3,5},{4,2},{5,3},{6,0},{7,1},{8,14},{9,15},{10,... | collective-permute-start | bytes 737288 | tf_op jit(solution)/shard_map/ppermute | solution.py:443
  143.2 1.0 collective-permute-start.19
  144.2 0.3 collective-permute-start.20
  144.6 1.3 collective-permute-start.21
  145.9 4.9 %collective-permute-done.18 = bf16[960,128]{1,0:T(8,128)(2,1)S(1)} collective-permute-done((bf16[960,128]{1,0:T(8,128)(2,1)S(1)}, bf16[960,128]{1,0:T(8,128)(2,1)S(1)}, u32[]{:S(2)}, u32[]{:S(2)}) %collective-permute-start.18) | collective-permute-done | bytes 245792 | tf_op jit(solution)/shard_map/ppermute | solution.py:443
  150.8 3.2 %collective-permute-done.19 = bf16[960,128]{1,0:T(8,128)(2,1)S(1)} collective-permute-done((bf16[960,128]{1,0:T(8,128)(2,1)S(1)}, bf16[960,128]{1,0:T(8,128)(2,1)S(1)}, u32[]{:S(2)}, u32[]{:S(2)}) %collective-permute-start.19) | collective-permute-done | bytes 245792 | tf_op jit(solution)/shard_map/ppermute | solution.py:443
  154.3 1.1 copy-done.2
  155.9 1.1 pad_maximum_fusion.2
  156.9 2.2 %finish.1 = (f32[6912,128]{1,0:T(8,128)}, f32[256,256]{1,0:T(8,128)}, f32[1,256]{1,0:T(1,128)}) custom-call(s32[1]{0:T(128)} %bitcast.refs_0_.bit_ref, bf16[3840,128]{1,0:T(8,128)(2,1)S(1)} %pad_maximum_fusion.mine_ref, bf16[3840,128]{1,0:T(8,128)(2,1)S(1)} %collective-permute-done.22.theirs_ref), custom_call_target="tpu_custom_call" | custom-call | flops 3300000000 | bytes 10500000 | tf_op jit(solution)/shard_map/finish/pallas_call | solution.py:409
  (55 shorter events, 1.7 us)
Async XLA Ops:
  6.1 6.4 %copy-start.3 = (bf16[1,16,16,8,128]{4,3,2,1,0:T(8,128)(2,1)S(1)}, bf16[1,16,16,8,128]{4,3,2,1,0:T(8,128)(2,1)}, u32[]{:S(2)}) copy-start(bf16[1,16,16,8,128]{4,3,2,1,0:T(8,128)(2,1)} %param.13) | copy-start | bytes 1572868
  6.1 24.3 %all-to-all-start = ((bf16[16,144,256]{2,1,0:T(8,128)(2,1)}), bf16[16,144,256]{2,1,0:T(8,128)(2,1)S(1)}, u32[]{:S(2)}, u32[]{:S(2)}) async-start(bf16[16,144,256]{2,1,0:T(8,128)(2,1)} %pack.2), calls=%async_computation | async-start | bytes 2359296 | tf_op jit(solution)/shard_map/all_to_all | solution.py:504
  12.7 6.8 %collective-permute-start = (bf16[256,128]{1,0:T(8,128)(2,1)S(1)}, bf16[256,128]{1,0:T(8,128)(2,1)S(1)}, u32[]{:S(2)}, u32[]{:S(2)}) collective-permute-start(bf16[256,128]{1,0:T(8,128)(2,1)S(1)} %bitcast.76), channel_id=1, source_target_pairs={{1,0},{2,1},{3,2},{5,4},{6,5},{7,6},{9,8},{10,9},{11,10},{13,12},{... | collective-permute-start | bytes 196616 | tf_op jit(solution)/shard_map/ppermute | solution.py:435
  19.5 15.3 %copy-start.4 = (bf16[2304,128]{1,0:T(8,128)(2,1)}, bf16[2304,128]{1,0:T(8,128)(2,1)S(1)}, u32[]{:S(2)}) copy-start(bf16[2304,128]{1,0:T(8,128)(2,1)S(1)} %pad_maximum_fusion.1.refs_5_) | copy-start | bytes 1769476
  30.4 3.7 %copy-start.1 = (bf16[16,144,256]{2,1,0:T(8,128)(2,1)}, bf16[16,144,256]{2,1,0:T(8,128)(2,1)S(1)}, u32[]{:S(2)}) copy-start(bf16[16,144,256]{2,1,0:T(8,128)(2,1)S(1)} %all-to-all-done.refs_2_) | copy-start | bytes 3538948
  30.4 35.1 %all-to-all-start.1 = ((bf16[16,144,256]{2,1,0:T(8,128)(2,1)}), bf16[16,144,256]{2,1,0:T(8,128)(2,1)S(1)}, u32[]{:S(2)}, u32[]{:S(2)}) async-start(bf16[16,144,256]{2,1,0:T(8,128)(2,1)} %pack.3), calls=%async_computation.1 | async-start | bytes 2359296 | tf_op jit(solution)/shard_map/all_to_all | solution.py:504
  34.8 31.5 %collective-permute-start.1 = (bf16[2304,128]{1,0:T(8,128)(2,1)S(1)}, bf16[2304,128]{1,0:T(8,128)(2,1)S(1)}, u32[]{:S(2)}, u32[]{:S(2)}) collective-permute-start(bf16[2304,128]{1,0:T(8,128)(2,1)S(1)} %pad_maximum_fusion.1.refs_5_), channel_id=1, source_target_pairs={{0,16},{16,0},{1,17},{17,1},{2,18},{18,2},{3,19},{19,3},{4,20},{20... | collective-permute-start | bytes 1769480 | tf_op jit(solution)/shard_map/ppermute | solution.py:439
  65.5 1.0 copy-start
  66.3 0.8 copy-start.6
  89.7 3.6 %collective-permute-start.2 = (bf16[3456,128]{1,0:T(8,128)(2,1)}, bf16[3456,128]{1,0:T(8,128)(2,1)S(1)}, u32[]{:S(2)}, u32[]{:S(2)}) collective-permute-start(bf16[3456,128]{1,0:T(8,128)(2,1)} %get-tuple-element.38), channel_id=1, source_target_pairs={{0,1},{1,0},{2,3},{3,2},{4,5},{5,4},{6,7},{7,6},{8,9},{9,8},{10,11... | collective-permute-start | bytes 2654216 | tf_op jit(solution)/shard_map/ppermute | solution.py:443
  91.1 21.2 %collective-permute-start.3 = (bf16[1584,128]{1,0:T(8,128)(2,1)}, bf16[1584,128]{1,0:T(8,128)(2,1)S(1)}, u32[]{:S(2)}, u32[]{:S(2)}) collective-permute-start(bf16[1584,128]{1,0:T(8,128)(2,1)} %get-tuple-element.42), channel_id=1, source_target_pairs={{0,16},{16,0},{1,17},{17,1},{2,18},{18,2},{3,19},{19,3},{4,20},{20... | collective-permute-start | bytes 1216520 | tf_op jit(solution)/shard_map/ppermute | solution.py:439
  94.8 17.4 %collective-permute-start.4 = (bf16[864,128]{1,0:T(8,128)(2,1)S(1)}, bf16[864,128]{1,0:T(8,128)(2,1)S(1)}, u32[]{:S(2)}, u32[]{:S(2)}) collective-permute-start(bf16[864,128]{1,0:T(8,128)(2,1)S(1)} %get-tuple-element.68), channel_id=1, source_target_pairs={{0,2},{1,3},{2,0},{3,1},{4,6},{5,7},{6,4},{7,5},{8,10},{9,11},{10,... | collective-permute-start | bytes 663560 | tf_op jit(solution)/shard_map/ppermute | solution.py:443
  97.5 14.7 %collective-permute-start.5 = (bf16[864,128]{1,0:T(8,128)(2,1)S(1)}, bf16[864,128]{1,0:T(8,128)(2,1)S(1)}, u32[]{:S(2)}, u32[]{:S(2)}) collective-permute-start(bf16[864,128]{1,0:T(8,128)(2,1)S(1)} %get-tuple-element.67), channel_id=1, source_target_pairs={{0,4},{1,5},{2,6},{3,7},{4,0},{5,1},{6,2},{7,3},{8,12},{9,13},{10,... | collective-permute-start | bytes 663560 | tf_op jit(solution)/shard_map/ppermute | solution.py:443
  98.8 13.4 %collective-permute-start.6 = (bf16[864,128]{1,0:T(8,128)(2,1)S(1)}, bf16[864,128]{1,0:T(8,128)(2,1)S(1)}, u32[]{:S(2)}, u32[]{:S(2)}) collective-permute-start(bf16[864,128]{1,0:T(8,128)(2,1)S(1)} %get-tuple-element.66), channel_id=1, source_target_pairs={{0,6},{1,7},{2,4},{3,5},{4,2},{5,3},{6,0},{7,1},{8,14},{9,15},{10,... | collective-permute-start | bytes 663560 | tf_op jit(solution)/shard_map/ppermute | solution.py:443
  99.2 14.0 %copy-start.7 = (bf16[720,128]{1,0:T(8,128)(2,1)S(1)}, bf16[720,128]{1,0:T(8,128)(2,1)}, u32[]{:S(2)}) copy-start(bf16[720,128]{1,0:T(8,128)(2,1)} %get-tuple-element.50) | copy-start | bytes 552964
  113.2 1.3 collective-permute-start.7
  113.2 11.9 %collective-permute-start.11 = (bf16[720,128]{1,0:T(8,128)(2,1)S(1)}, bf16[720,128]{1,0:T(8,128)(2,1)S(1)}, u32[]{:S(2)}, u32[]{:S(2)}) collective-permute-start(bf16[720,128]{1,0:T(8,128)(2,1)S(1)} %copy-done.7), channel_id=1, source_target_pairs={{0,16},{16,0},{1,17},{17,1},{2,18},{18,2},{3,19},{19,3},{4,20},{20... | collective-permute-start | bytes 552968 | tf_op jit(solution)/shard_map/ppermute | solution.py:439
  115.4 5.1 %collective-permute-start.10 = (bf16[96,128]{1,0:T(8,128)(2,1)S(1)}, bf16[96,128]{1,0:T(8,128)(2,1)S(1)}, u32[]{:S(2)}, u32[]{:S(2)}) collective-permute-start(bf16[96,128]{1,0:T(8,128)(2,1)S(1)} %get-tuple-element.78), channel_id=1, source_target_pairs={{0,6},{1,7},{2,4},{3,5},{4,2},{5,3},{6,0},{7,1},{8,14},{9,15},{10,... | collective-permute-start | bytes 73736 | tf_op jit(solution)/shard_map/ppermute | solution.py:443
  118.7 3.8 %collective-permute-start.8 = (bf16[96,128]{1,0:T(8,128)(2,1)S(1)}, bf16[96,128]{1,0:T(8,128)(2,1)S(1)}, u32[]{:S(2)}, u32[]{:S(2)}) collective-permute-start(bf16[96,128]{1,0:T(8,128)(2,1)S(1)} %get-tuple-element.77), channel_id=1, source_target_pairs={{0,2},{1,3},{2,0},{3,1},{4,6},{5,7},{6,4},{7,5},{8,10},{9,11},{10,... | collective-permute-start | bytes 73736 | tf_op jit(solution)/shard_map/ppermute | solution.py:443
  119.0 18.6 %copy-start.5 = (f32[256,128]{1,0:T(8,128)S(1)}, f32[256,128]{1,0:T(8,128)}, u32[]{:S(2)}) copy-start(f32[256,128]{1,0:T(8,128)} %get-tuple-element.54) | copy-start | bytes 393220
  119.0 3.8 %collective-permute-start.9 = (bf16[96,128]{1,0:T(8,128)(2,1)S(1)}, bf16[96,128]{1,0:T(8,128)(2,1)S(1)}, u32[]{:S(2)}, u32[]{:S(2)}) collective-permute-start(bf16[96,128]{1,0:T(8,128)(2,1)S(1)} %get-tuple-element.79), channel_id=1, source_target_pairs={{0,4},{1,5},{2,6},{3,7},{4,0},{5,1},{6,2},{7,3},{8,12},{9,13},{10,... | collective-permute-start | bytes 73736 | tf_op jit(solution)/shard_map/ppermute | solution.py:443
  125.1 4.6 %collective-permute-start.12 = (bf16[240,128]{1,0:T(8,128)(2,1)S(1)}, bf16[240,128]{1,0:T(8,128)(2,1)S(1)}, u32[]{:S(2)}, u32[]{:S(2)}) collective-permute-start(bf16[240,128]{1,0:T(8,128)(2,1)S(1)} %get-tuple-element.74), channel_id=1, source_target_pairs={{0,8},{1,9},{2,10},{3,11},{4,12},{5,13},{6,14},{7,15},{8,0},{9,1},... | collective-permute-start | bytes 184328 | tf_op jit(solution)/shard_map/ppermute | solution.py:443
  125.2 7.8 %collective-permute-start.13 = (bf16[240,128]{1,0:T(8,128)(2,1)S(1)}, bf16[240,128]{1,0:T(8,128)(2,1)S(1)}, u32[]{:S(2)}, u32[]{:S(2)}) collective-permute-start(bf16[240,128]{1,0:T(8,128)(2,1)S(1)} %get-tuple-element.76), channel_id=1, source_target_pairs={{0,16},{1,17},{2,18},{3,19},{4,20},{5,21},{6,22},{7,23},{8,24},{9,... | collective-permute-start | bytes 184328 | tf_op jit(solution)/shard_map/ppermute | solution.py:443
  126.9 6.1 %collective-permute-start.14 = (bf16[240,128]{1,0:T(8,128)(2,1)S(1)}, bf16[240,128]{1,0:T(8,128)(2,1)S(1)}, u32[]{:S(2)}, u32[]{:S(2)}) collective-permute-start(bf16[240,128]{1,0:T(8,128)(2,1)S(1)} %get-tuple-element.75), channel_id=1, source_target_pairs={{0,24},{1,25},{2,26},{3,27},{4,28},{5,29},{6,30},{7,31},{8,16},{9,... | collective-permute-start | bytes 184328 | tf_op jit(solution)/shard_map/ppermute | solution.py:443
  133.1 6.3 %collective-permute-start.15 = (bf16[240,128]{1,0:T(8,128)(2,1)S(1)}, bf16[240,128]{1,0:T(8,128)(2,1)S(1)}, u32[]{:S(2)}, u32[]{:S(2)}) collective-permute-start(bf16[240,128]{1,0:T(8,128)(2,1)S(1)} %fusion.4), channel_id=1, source_target_pairs={{0,24},{1,25},{2,26},{3,27},{4,28},{5,29},{6,30},{7,31},{8,16},{9,... | collective-permute-start | bytes 184328 | tf_op jit(solution)/shard_map/ppermute | solution.py:443
  135.8 5.1 %collective-permute-start.16 = (bf16[240,128]{1,0:T(8,128)(2,1)S(1)}, bf16[240,128]{1,0:T(8,128)(2,1)S(1)}, u32[]{:S(2)}, u32[]{:S(2)}) collective-permute-start(bf16[240,128]{1,0:T(8,128)(2,1)S(1)} %fusion.4), channel_id=1, source_target_pairs={{0,16},{1,17},{2,18},{3,19},{4,20},{5,21},{6,22},{7,23},{8,24},{9,... | collective-permute-start | bytes 184328 | tf_op jit(solution)/shard_map/ppermute | solution.py:443
  135.8 5.1 %collective-permute-start.17 = (bf16[240,128]{1,0:T(8,128)(2,1)S(1)}, bf16[240,128]{1,0:T(8,128)(2,1)S(1)}, u32[]{:S(2)}, u32[]{:S(2)}) collective-permute-start(bf16[240,128]{1,0:T(8,128)(2,1)S(1)} %fusion.4), channel_id=1, source_target_pairs={{0,8},{1,9},{2,10},{3,11},{4,12},{5,13},{6,14},{7,15},{8,0},{9,1},... | collective-permute-start | bytes 184328 | tf_op jit(solution)/shard_map/ppermute | solution.py:443
  141.0 9.9 %collective-permute-start.18 = (bf16[960,128]{1,0:T(8,128)(2,1)S(1)}, bf16[960,128]{1,0:T(8,128)(2,1)S(1)}, u32[]{:S(2)}, u32[]{:S(2)}) collective-permute-start(bf16[960,128]{1,0:T(8,128)(2,1)S(1)} %pad_maximum_fusion.4), channel_id=1, source_target_pairs={{0,6},{1,7},{2,4},{3,5},{4,2},{5,3},{6,0},{7,1},{8,14},{9,15},{10,... | collective-permute-start | bytes 737288 | tf_op jit(solution)/shard_map/ppermute | solution.py:443
  143.2 10.8 %collective-permute-start.19 = (bf16[960,128]{1,0:T(8,128)(2,1)S(1)}, bf16[960,128]{1,0:T(8,128)(2,1)S(1)}, u32[]{:S(2)}, u32[]{:S(2)}) collective-permute-start(bf16[960,128]{1,0:T(8,128)(2,1)S(1)} %pad_maximum_fusion.4), channel_id=1, source_target_pairs={{0,4},{1,5},{2,6},{3,7},{4,0},{5,1},{6,2},{7,3},{8,12},{9,13},{10,... | collective-permute-start | bytes 737288 | tf_op jit(solution)/shard_map/ppermute | solution.py:443
  144.2 9.8 %collective-permute-start.20 = (bf16[960,128]{1,0:T(8,128)(2,1)S(1)}, bf16[960,128]{1,0:T(8,128)(2,1)S(1)}, u32[]{:S(2)}, u32[]{:S(2)}) collective-permute-start(bf16[960,128]{1,0:T(8,128)(2,1)S(1)} %pad_maximum_fusion.4), channel_id=1, source_target_pairs={{0,2},{1,3},{2,0},{3,1},{4,6},{5,7},{6,4},{7,5},{8,10},{9,11},{10,... | collective-permute-start | bytes 737288 | tf_op jit(solution)/shard_map/ppermute | solution.py:443
  144.6 9.6 %collective-permute-start.21 = (f32[256,128]{1,0:T(8,128)S(1)}, f32[256,128]{1,0:T(8,128)S(1)}, u32[]{:S(2)}, u32[]{:S(2)}) collective-permute-start(f32[256,128]{1,0:T(8,128)S(1)} %convert_add_fusion.1), channel_id=1, source_target_pairs={{0,1},{1,2},{2,3},{4,5},{5,6},{6,7},{8,9},{9,10},{10,11},{12,13},{... | collective-permute-start | bytes 393224 | tf_op jit(solution)/shard_map/ppermute | solution.py:435
  154.2 1.2 copy-start.2
  154.3 2.7 %collective-permute-start.22 = (bf16[3840,128]{1,0:T(8,128)(2,1)S(1)}, bf16[3840,128]{1,0:T(8,128)(2,1)S(1)}, u32[]{:S(2)}, u32[]{:S(2)}) collective-permute-start(bf16[3840,128]{1,0:T(8,128)(2,1)S(1)} %pad_maximum_fusion.mine_ref), channel_id=1, source_target_pairs={{0,1},{1,0},{2,3},{3,2},{4,5},{5,4},{6,7},{7,6},{8,9},{9,8},{10,11... | collective-permute-start | bytes 2949128 | tf_op jit(solution)/shard_map/ppermute | solution.py:443
